TPU v7x, 32 devices: a whole 2x2x4 slice. The times are simulated.
32 devices in a mesh: box: 8 (over y, x, core), grp: 4 (over z).
Axes of the slice: x: 2, y: 2, z: 4, core: 2. Of those that a mesh axis runs over, the one named last changes fastest.
Arguments:
- source: bfloat16 [5120, 32, 32], P(('box', 'grp')), may hold values from -6 to 6
- conductivity: bfloat16 [5120, 32, 32], P(('box', 'grp')), may hold values from 0.25 to 4
- new_owner: int32 [8, 4, 5, 1], P('box', 'grp'), may hold values from 0 to 3; in each aligned block of 5 rows (0 to 4, 5 to 9, ..., all dimensions but the last counted through in order) at most 3 rows name the same one
Outputs:
- correction: bfloat16 [8, 4, 4, 3, 32768], P('box', 'grp')
- coarse_residual: float32 [4, 40, 4096], P('grp')
Inputs may be any that keep to these rules, and one draw needn't show every extreme that they name: `new_owner`: boxes move only within their box index; among the 5 boxes of one device at most 3 share a new owner, and in every draw some device gives exactly 3 boxes to one owner.
All inputs are finite; a program needn't handle non-finite values.
Results may differ from a plain program's by a relative error of at most 0.001.
Values may be sent and summed in bfloat16 or wider, within the bound.
A program may use at most 128 MiB of HBM per device.

v0:
```python
import jax
import jax.numpy as jnp
from jax import lax
from jax.sharding import PartitionSpec as P

WEIGHT = 0.8


def padded_2(cells, sides, width):
    for axis, dim in sides:
        count = lax.axis_size(axis)
        ends = count - 1
        head = lax.slice_in_dim(cells, 0, width, axis=dim)
        tail = lax.slice_in_dim(cells, cells.shape[dim] - width, cells.shape[dim], axis=dim)
        cells = jnp.concatenate(
            [
                lax.ppermute(tail, axis, [(i, (i + 1) % count) for i in range(ends)]),
                cells,
                lax.ppermute(head, axis, [((i + 1) % count, i) for i in range(ends)]),
            ],
            axis=dim,
        )
    return cells


def shift_next(values_in, which):
    extent = values_in.shape[which]
    widths = [(0, 0)] * values_in.ndim
    widths[which] = (0, 1)
    return jnp.pad(lax.slice_in_dim(values_in, 1, extent, axis=which), widths)


def shift_prev(values_in, which):
    extent = values_in.shape[which]
    widths = [(0, 0)] * values_in.ndim
    widths[which] = (1, 0)
    return jnp.pad(lax.slice_in_dim(values_in, 0, extent - 1, axis=which), widths)


def smooth(source, conductivity):
    inside = conductivity > 0
    axes_list = (conductivity.ndim - 3, conductivity.ndim - 2, conductivity.ndim - 1)
    face_list = []
    diagonal = jnp.zeros_like(conductivity)
    for which in axes_list:
        after = shift_next(conductivity, which)
        face_fwd = jnp.where(inside & (after > 0), 0.5 * (conductivity + after), 0.0)
        face_list.append(face_fwd)
        before = shift_prev(conductivity, which)
        face_bwd = shift_prev(face_fwd, which)
        diagonal = diagonal + jnp.where(after > 0, face_fwd, conductivity)
        diagonal = diagonal + jnp.where(before > 0, face_bwd, conductivity)
    divisor = jnp.where(inside, diagonal, 1.0)

    def operate(values_in):
        result = diagonal * values_in
        for which, face_fwd in zip(axes_list, face_list):
            result = result - face_fwd * shift_next(values_in, which)
            result = result - shift_prev(face_fwd * values_in, which)
        return result

    sweep_one = jnp.where(inside, WEIGHT * source / divisor, 0.0)
    sweep_two = jnp.where(inside, sweep_one + WEIGHT * (source - operate(sweep_one)) / divisor, 0.0)
    leftover = jnp.where(inside, source - operate(sweep_two), 0.0)
    return (sweep_two, leftover)


def restrict(leftover):
    leading = leftover.shape[:-3]
    layers, rows_y, rows_x = leftover.shape[-3:]
    blocks = leftover.reshape(leading + (layers // 2, 2, rows_y // 2, 2, rows_x // 2, 2))
    return jnp.mean(blocks, axis=(-5, -3, -1)).reshape(leading + (-1,))


def ranks_of(owners):
    count = owners.shape[-1]
    order = jnp.arange(count)
    earlier = (owners[..., :, None] == owners[..., None, :]) & (order[:, None] < order[None, :])
    return jnp.sum(earlier.astype(jnp.int32), axis=-2)


def shards(source, conductivity, new_owner):
    total_layers, rows_y, rows_x = source.shape
    box_count = new_owner.shape[2]
    layers = total_layers // box_count
    box_cells = layers * rows_y * rows_x
    group_count = lax.axis_size("grp")
    slots_per = max(2, (2 * box_count + group_count - 1) // group_count)
    stacked = jnp.stack([source, conductivity])
    padded = padded_2(stacked, ((("box", "grp"), 1),), 3)
    sweep_two, leftover = smooth(padded[0].astype(jnp.float32), padded[1].astype(jnp.float32))
    settled = sweep_two[3 : 3 + total_layers].reshape(box_count, box_cells).astype(jnp.bfloat16)
    restricted = restrict(leftover[3 : 3 + total_layers].reshape(box_count, layers, rows_y, rows_x))
    owners = new_owner.reshape(box_count)
    gathered, owner_list = (
        lax.all_gather(settled, "grp", axis=0, tiled=True),
        lax.all_gather(owners.astype(jnp.bfloat16), "grp", axis=0, tiled=True),
    )
    owner_ids = owner_list.astype(jnp.int32).reshape(group_count, box_count)
    rank_all = ranks_of(owner_ids)
    mine = owner_ids == lax.axis_index("grp")
    slot_ids = jnp.arange(slots_per, dtype=jnp.int32)
    select = (mine[:, :, None] & (rank_all[:, :, None] == slot_ids[None, None, :])).astype(
        jnp.bfloat16
    )
    boxes = gathered.reshape(group_count, box_count, box_cells)
    received = jnp.einsum("gkr,gkc->grc", select, boxes, preferred_element_type=jnp.float32).astype(
        jnp.bfloat16
    )
    coarse = lax.all_gather(restricted, "box", axis=0, tiled=True)
    return (
        received.reshape(1, 1, group_count, slots_per, box_cells),
        coarse.reshape(1, coarse.shape[0], coarse.shape[1]),
    )


def solution(mesh):
    placed = (
        P(("box", "grp"), None, None),
        P(("box", "grp"), None, None),
        P("box", "grp", None, None),
    )
    return jax.shard_map(
        shards,
        mesh=mesh,
        in_specs=placed,
        out_specs=(P("box", "grp", None, None, None), P("grp", None, None)),
        check_vma=False,
    )
```

profile of v0, /device:TPU:0, one launch (start us, length us, event | category | flops | bytes accessed | tf_op | source)
XLA Modules:
  0.0 127.6 jit_solution(11876193806280352048)
XLA Ops:
  7.2 0.0 copy-start.8
  7.2 0.0 all-gather.5.cloned.1.call-start
  7.3 1.5 %fusion.3 = (bf16[2,3,32,32]{1,3,2,0:T(8,128)(2,1)S(1)}, bf16[2,3,32,32]{1,3,2,0:T(8,128)(2,1)S(1)}) fusion(bf16[1,160,32,32]{1,3,2,0:T(8,128)(2,1)} %bitcast.43, bf16[1,160,32,32]{1,3,2,0:T(8,128)(2,1)} %bitcast.45), kind=kLoop, calls=%fused_computation.35 | loop fusion | flops 49152 | bytes 679936 | tf_op jit(solution)/shard_map/stack | solution.py:89
  8.7 5.0 %collective-permute-start = (bf16[2,3,32,32]{1,3,2,0:T(8,128)(2,1)S(1)}, bf16[2,3,32,32]{1,3,2,0:T(8,128)(2,1)S(1)}, u32[]{:S(2)}, u32[]{:S(2)}) collective-permute-start(bf16[2,3,32,32]{1,3,2,0:T(8,128)(2,1)S(1)} %get-tuple-element.39), channel_id=1, source_target_pairs={{0,1},{1,2},{2,3},{3,4},{4,5},{5,6},{6,7},{7,8},{8,9},{9,10},{10,1... | collective-permute-start | bytes 36872 | tf_op jit(solution)/shard_map/ppermute | solution.py:17
  13.7 1.3 %collective-permute-start.1 = (bf16[2,3,32,32]{1,3,2,0:T(8,128)(2,1)S(1)}, bf16[2,3,32,32]{1,3,2,0:T(8,128)(2,1)S(1)}, u32[]{:S(2)}, u32[]{:S(2)}) collective-permute-start(bf16[2,3,32,32]{1,3,2,0:T(8,128)(2,1)S(1)} %get-tuple-element.40), channel_id=1, source_target_pairs={{1,0},{2,1},{3,2},{4,3},{5,4},{6,5},{7,6},{8,7},{9,8},{10,9},{11,1... | collective-permute-start | bytes 36872 | tf_op jit(solution)/shard_map/ppermute | solution.py:19
  15.0 0.0 copy-done.7
  15.1 0.6 dynamic-slice
  16.3 0.2 dynamic-update-slice
  16.6 24.7 %all-reduce.21 = bf16[20]{0:T(256)(128)(2,1)S(1)} all-reduce(bf16[20]{0:T(256)(128)(2,1)S(1)} %dynamic-update-slice), channel_id=2, replica_groups=mesh['box'=8,'grp'=4] {'grp'}, use_global_device_ids=true, to_apply=%add.21 | all-reduce | flops 20 | bytes 80
  41.2 0.1 reshape.58
  41.3 0.1 copy.16
  41.4 0.1 convert_reduce_fusion
  41.5 0.0 collective-permute-done
  41.5 0.0 collective-permute-done.1
  41.6 0.7 pad_maximum_fusion
  42.3 1.2 fusion.4
  43.5 0.2 fusion.16
  43.7 0.2 fusion.17
  43.9 0.4 slice_bitcast_fusion
  44.3 0.4 multiply_select_fusion.2
  44.7 0.6 multiply_select_fusion.1
  45.3 0.1 slice.144
  45.4 1.8 %divide_select_fusion = (f32[166,32,32]{0,2,1:T(8,128)S(1)}, f32[166,32,32]{0,2,1:T(8,128)S(1)}) fusion(pred[166,32,32]{0,2,1:T(8,128)(4,1)S(1)} %get-tuple-element.15, bf16[2,166,32,32]{1,3,2,0:T(8,128)(2,1)S(1)} %pad_maximum_fusion, f32[166,32,31]{0,2,1:T(8,128)S(1)} %bitcast.41, f32[166,32,31]{0,2,1:T(8,128)S(1)} %get-tuple-element.37, ...), kind=kLoop, calls=%fused_computation.22 | loop fusion | flops 3909632 | bytes 10229248 | tf_op jit(solution)/shard_map/jit(_where)/select_n | solution.py:62
  47.2 0.3 fusion.14
  47.5 0.3 fusion.15
  47.8 0.4 fusion.13
  48.3 1.5 %add_select_fusion = f32[166,32,32]{0,2,1:T(8,128)S(1)} fusion(pred[166,32,32]{0,2,1:T(8,128)(4,1)S(1)} %get-tuple-element.15, f32[166,32,31]{0,2,1:T(8,128)S(1)} %get-tuple-element.32, f32[166,32,32]{0,2,1:T(8,128)S(1)} %get-tuple-element.17, f32[166,32,31]{0,2,1:T(8,128)S(1)} %get-tuple-element.31, f32[166,31,32]{0,2,1:T(8,128)S(1)} %get-tuple-element.30, ...), kind=kLoop, calls=%fused_computation.21 | loop fusion | flops 3399680 | bytes 7896064 | tf_op jit(solution)/shard_map/jit(_where)/select_n | solution.py:63
  49.7 1.0 slice.204
  50.8 2.8 %copy.17 = bf16[160,32,32]{2,1,0:T(8,128)(2,1)} copy(bf16[160,32,32]{0,2,1:T(8,128)(2,1)} %slice.204) | data formatting | bytes 655360 | tf_op jit(solution)/shard_map/slice | solution.py:92
  53.5 3.4 %reshape.67 = bf16[1,5,32768]{2,1,0:T(8,128)(2,1)} reshape(bf16[160,32,32]{2,1,0:T(8,128)(2,1)} %copy.17) | data formatting | bytes 655360
  57.0 0.0 all-gather.5.cloned.1.call-update
  57.0 1.4 %fusion.11 = (f32[166,31,32]{0,2,1:T(8,128)S(1)}, f32[166,31,32]{0,2,1:T(8,128)S(1)}) fusion(f32[166,32,32]{0,2,1:T(8,128)S(1)} %add_select_fusion, f32[166,32,32]{0,2,1:T(8,128)} %copy-done), kind=kLoop, calls=%fused_computation.53 | loop fusion | flops 164672 | bytes 3293440 | tf_op jit(solution)/shard_map/slice | solution.py:30
  58.4 0.2 fusion.12
  58.6 0.4 fusion.10
  59.1 0.8 copy-done.1
  59.8 0.3 copy-done.3
  60.2 0.9 pad_multiply_fusion.1
  61.1 0.3 copy-done.4
  61.4 2.3 %fusion.1 = f32[160,32,32]{0,2,1:T(8,128)S(1)} fusion(f32[166,32,32]{0,2,1:T(8,128)S(1)} %copy-done.4, f32[166,32,31]{0,2,1:T(8,128)S(1)} %get-tuple-element.23, f32[166,32,31]{0,2,1:T(8,128)S(1)} %get-tuple-element.22, f32[166,32,32]{0,2,1:T(8,128)S(1)} %get-tuple-element.17, f32[166,31,32]{0,2,1:T(8,128)S(1)} %get-tuple-element.21, ...), kind=kLoop, calls=%fused_computation.3 | loop fusion | flops 1146880 | bytes 5416704 | tf_op jit(solution)/shard_map/jit(_where)/select_n | solution.py:64
  63.6 23.9 %reshape_reshape.3 = f32[5,16,2,16,2,16,2]{2,1,0,6,5,4,3:T(8,128)} reshape(f32[160,32,32]{0,2,1:T(8,128)S(1)} %fusion.1) | data formatting | bytes 1310720 | tf_op jit(solution)/shard_map/reshape;reshape | solution.py:71
  87.6 15.4 %reduce_sum.19 = f32[5,16,16,16]{1,0,3,2:T(8,128)S(1)} reduce(f32[5,16,2,16,2,16,2]{2,1,0,6,5,4,3:T(8,128)} %reshape_reshape.3, f32[]{:T(128)} %constant.3.clone.1), dimensions={2,4,6}, to_apply=%region_1.2 | reduce | flops 143360 | bytes 737284 | tf_op jit(solution)/shard_map/reduce_sum | solution.py:72
  102.9 0.4 copy.18
  103.3 0.1 broadcast_multiply_fusion
  103.4 0.3 reshape.69
  103.7 12.2 %all-gather.2 = f32[8,5,4096]{2,1,0:T(8,128)S(1)} all-gather(f32[1,5,4096]{2,1,0:T(8,128)S(1)} %reshape.69), channel_id=1, replica_groups=mesh['box'=8,'grp'=4] {'box'}, dimensions={0}, use_global_device_ids=true | all-gather | bytes 737280 | tf_op jit(solution)/shard_map/all_gather | solution.py:110
  115.9 1.0 reshape.56
  116.9 2.3 %fusion = bf16[1,1,4,3,32768]{4,3,2,1,0:T(4,128)(2,1)S(1)} fusion(bf16[4,5,32768]{2,1,0:T(8,128)(2,1)} %all-gather.5.cloned.1.call-done, s32[4,5]{1,0:T(4,128)S(1)} %convert_reduce_fusion, pred[4,5]{1,0:T(4,128)(4,1)S(1)} %broadcast_compare_fusion.1), kind=kOutput, calls=%fused_computation.1 | convolution fusion | flops 4325496 | bytes 2097252 | tf_op jit(solution)/shard_map/gkr,gkc->grc/dot_general | solution.py:107
  119.2 1.6 %copy.19 = bf16[1,1,4,3,32768]{4,2,3,1,0:T(4,128)(2,1)} copy(bf16[1,1,4,3,32768]{4,3,2,1,0:T(4,128)(2,1)S(1)} %fusion) | data formatting | bytes 1572864
  (19 shorter events, 0.1 us)
Async XLA Ops:
  7.2 7.9 %copy-start.8 = (u32[32]{0:T(128)S(1)}, u32[32]{0:T(128)}, u32[]{:S(2)}) copy-start(u32[32]{0:T(128)} %constant.64) | copy-start | bytes 388
  7.2 34.4 %copy-start.6 = (bf16[160,32,32]{0,2,1:T(8,128)(2,1)S(1)}, bf16[160,32,32]{0,2,1:T(8,128)(2,1)}, u32[]{:S(2)}) copy-start(bf16[160,32,32]{0,2,1:T(8,128)(2,1)} %param.4) | copy-start | bytes 983044
  7.2 34.4 %copy-start.5 = (bf16[160,32,32]{0,2,1:T(8,128)(2,1)S(1)}, bf16[160,32,32]{0,2,1:T(8,128)(2,1)}, u32[]{:S(2)}) copy-start(bf16[160,32,32]{0,2,1:T(8,128)(2,1)} %param.3) | copy-start | bytes 983044
  7.2 7.8 %copy-start.7 = (s32[1,1,5,1]{2,3,1,0:T(1,128)S(1)}, s32[1,1,5,1]{2,3,1,0:T(1,128)}, u32[]{:S(2)}) copy-start(s32[1,1,5,1]{2,3,1,0:T(1,128)} %param.5) | copy-start | bytes 64
  7.2 109.7 %all-gather.5.cloned.1.call-start = ((), (), s32[]{:S(2)}) async-start(), calls=%async_computation | async-start | bytes 2621440 | tf_op jit(solution)/shard_map/all_gather | solution.py:96
  8.7 32.8 %collective-permute-start = (bf16[2,3,32,32]{1,3,2,0:T(8,128)(2,1)S(1)}, bf16[2,3,32,32]{1,3,2,0:T(8,128)(2,1)S(1)}, u32[]{:S(2)}, u32[]{:S(2)}) collective-permute-start(bf16[2,3,32,32]{1,3,2,0:T(8,128)(2,1)S(1)} %get-tuple-element.39), channel_id=1, source_target_pairs={{0,1},{1,2},{2,3},{3,4},{4,5},{5,6},{6,7},{7,8},{8,9},{9,10},{10,1... | collective-permute-start | bytes 36872 | tf_op jit(solution)/shard_map/ppermute | solution.py:17
  13.7 27.8 %collective-permute-start.1 = (bf16[2,3,32,32]{1,3,2,0:T(8,128)(2,1)S(1)}, bf16[2,3,32,32]{1,3,2,0:T(8,128)(2,1)S(1)}, u32[]{:S(2)}, u32[]{:S(2)}) collective-permute-start(bf16[2,3,32,32]{1,3,2,0:T(8,128)(2,1)S(1)} %get-tuple-element.40), channel_id=1, source_target_pairs={{1,0},{2,1},{3,2},{4,3},{5,4},{6,5},{7,6},{8,7},{9,8},{10,9},{11,1... | collective-permute-start | bytes 36872 | tf_op jit(solution)/shard_map/ppermute | solution.py:19
  45.3 2.9 %copy-start = (f32[166,32,32]{0,2,1:T(8,128)}, f32[166,32,32]{0,2,1:T(8,128)S(1)}, u32[]{:S(2)}) copy-start(f32[166,32,32]{0,2,1:T(8,128)S(1)} %get-tuple-element.16) | copy-start | bytes 2039812
  47.2 1.1 copy-start.2
  58.6 1.2 copy-start.1
  58.6 1.5 %copy-start.3 = (f32[166,32,32]{0,2,1:T(8,128)S(1)}, f32[166,32,32]{0,2,1:T(8,128)}, u32[]{:S(2)}) copy-start(f32[166,32,32]{0,2,1:T(8,128)} %copy-done.2) | copy-start | bytes 2039812
  60.2 1.2 copy-start.4
Sparse Core Ops, SparseCore 0:
  57.1 45.3 all-gather.4
where the time goes:
time: 128 us
  local copies, waits for them, and re-layouts  37.8 us (30%)
  blocking collectives  36.9 us (29%)
  other arithmetic  29.4 us (23%)
  between operations  15 us (12%)
  starting transfers between devices  6.29 us (5%)
  matrix products  2.28 us (2%)
    unnamed x1, blocking collectives  24.7 us
    another operation x1, local copies, waits for them, and re-layouts, restrict(): leftover.reshape(leading + (layers // 2, 2, rows_y // 2, 2, rows_x // 2, 2))  23.9 us
    reduce_sum x1, other arithmetic, restrict(): return jnp.mean(blocks, axis=(-5, -3, -1)).reshape(leading + (-1,))  15.4 us
    all_gather x1, blocking collectives, shards(): coarse = lax.all_gather(restricted, 'box', axis=0, tiled=True)  12.2 us
    unnamed x24, local copies, waits for them, and re-layouts  7.63 us
    ppermute x1, starting transfers between devices, padded_2(): lax.ppermute(tail, axis, [(i, (i + 1) % count) for i in range(ends)])  4.96 us
    slice x2, local copies, waits for them, and re-layouts, shards(): sweep_two[3:3 + total_layers].reshape(box_count, box_cells)  3.8 us
    slice x6, other arithmetic, shift_next(): return jnp.pad(lax.slice_in_dim(values_in, 1, extent, axis=which), widths)  3.04 us
  transfers between devices with their start and end apart: 3, of which 0 were waited for; matrix products, arithmetic and copies ran while one was open for 37% of the time, Pallas kernels for 0%

commit v1 on v0

v1 whole, which is shorter than its diff:
```python
import functools

import jax
import jax.numpy as jnp
from jax import lax
from jax.experimental import pallas as pl
from jax.experimental.pallas import tpu as pltpu
from jax.sharding import PartitionSpec as P

WEIGHT = 0.8
HALO = 3
STEP = 8
MESH = pl.DeviceIdType.MESH


def lane_sub(shape):
    lane = lax.broadcasted_iota(jnp.int32, shape, len(shape) - 1)
    sub = lax.broadcasted_iota(jnp.int32, shape, len(shape) - 2)
    return lane, sub


def y_next(v):
    lane, _ = lane_sub(v.shape)
    a = pltpu.roll(v, 96, 2)
    return jnp.where(lane < 96, a, pltpu.roll(a, 7, 1))


def y_prev(v):
    lane, _ = lane_sub(v.shape)
    a = pltpu.roll(v, 32, 2)
    return jnp.where(lane >= 32, a, pltpu.roll(a, 1, 1))


def x_next(v):
    return pltpu.roll(v, 127, 2)


def x_prev(v):
    return pltpu.roll(v, 1, 2)


def kernel(
    sizes,
    owner_ref,
    source_ref,
    cond_ref,
    corr_ref,
    coarse_ref,
    fc,
    ax_s,
    ay_s,
    az_s,
    inv_s,
    u1_s,
    u2_s,
    t_s,
    boxes,
    slots,
    rs,
    res,
    coarse_s,
    halo_send,
    halo_recv,
    corr_send,
    corr_recv,
    coarse_send,
    coarse_recv,
    local_sem,
):
    n_box, n_grp, nb, layers, ranks = sizes
    total = nb * layers
    me_s, me_g = lax.axis_index("box"), lax.axis_index("grp")
    me = me_s * n_grp + me_g
    count = n_box * n_grp
    after = lax.rem(me + 1, count)
    before = lax.rem(me + count - 1, count)
    after_id = (after // n_grp, lax.rem(after, n_grp))
    before_id = (before // n_grp, lax.rem(before, n_grp))

    barrier = pltpu.get_barrier_semaphore()
    for target in (after_id, before_id):
        pl.semaphore_signal(barrier, inc=1, device_id=target, device_id_type=MESH)

    def greet_grp(off, carry):
        target = (me_s, lax.rem(me_g + off, n_grp))
        pl.semaphore_signal(barrier, inc=1, device_id=target, device_id_type=MESH)
        return carry

    def greet_box(off, carry):
        target = (lax.rem(me_s + off, n_box), me_g)
        pl.semaphore_signal(barrier, inc=1, device_id=target, device_id_type=MESH)
        return carry

    lax.fori_loop(1, n_grp, greet_grp, 0)
    lax.fori_loop(1, n_box, greet_box, 0)

    eye = jnp.where(
        lax.broadcasted_iota(jnp.int32, (total, total), 0)
        == lax.broadcasted_iota(jnp.int32, (total, total), 1),
        1.0,
        0.0,
    ).astype(jnp.bfloat16)
    for which, ref in enumerate((source_ref, cond_ref)):
        for b in range(4):
            turned = lax.dot_general(
                eye,
                ref[pl.ds(b * 256, 256)],
                (((1,), (1,)), ((), ())),
                preferred_element_type=jnp.float32,
            )
            for h in range(2):
                fc[which, pl.ds(HALO * 8 + 2 * b + h, total, stride=8), :] = turned[
                    :, h * 128 : (h + 1) * 128
                ]

    pl.semaphore_wait(barrier, n_grp + n_box)
    to_after = pltpu.make_async_remote_copy(
        src_ref=fc.at[:, pl.ds(total * 8, HALO * 8)],
        dst_ref=fc.at[:, pl.ds(0, HALO * 8)],
        send_sem=halo_send.at[0],
        recv_sem=halo_recv.at[0],
        device_id=after_id,
        device_id_type=MESH,
    )
    to_before = pltpu.make_async_remote_copy(
        src_ref=fc.at[:, pl.ds(HALO * 8, HALO * 8)],
        dst_ref=fc.at[:, pl.ds((total + HALO) * 8, HALO * 8)],
        send_sem=halo_send.at[1],
        recv_sem=halo_recv.at[1],
        device_id=before_id,
        device_id_type=MESH,
    )
    to_after.start()
    to_before.start()

    def field(which, start, n):
        return fc[which, pl.ds(pl.multiple_of(start * 8, 8), n * 8)].reshape(n, 8, 128)

    def first(start, n):
        lane, sub = lane_sub((1, 8, 128))
        x = lane % 32
        y = sub * 4 + lane // 32
        half_x = jnp.where(x != 31, 0.5, 0.0)
        half_y = jnp.where(y != 31, 0.5, 0.0)
        sides = (
            jnp.where(x == 0, 1.0, 0.0)
            + jnp.where(x == 31, 1.0, 0.0)
            + jnp.where(y == 0, 1.0, 0.0)
            + jnp.where(y == 31, 1.0, 0.0)
        )
        slab = field(1, start - 1, n + 2)
        c = slab[1:-1]
        az = 0.5 * (slab[1:] + slab[:-1])
        ax = half_x * (c + x_next(c))
        ay = half_y * (c + y_next(c))
        diag = ax + x_prev(ax) + ay + y_prev(ay) + az[1:] + az[:-1] + sides * c
        inv = WEIGHT / diag
        here = pl.ds(start, n)
        ax_s[here] = ax
        ay_s[here] = ay
        az_s[here] = az[1:]
        inv_s[here] = inv
        u1_s[here] = inv * field(0, start, n)

    def first_step(i, carry):
        first(HALO + i * STEP, STEP)
        return carry

    last = total // STEP - 1
    lax.fori_loop(1, last, first_step, 0, unroll=2)

    def own_slots():
        owners = [owner_ref[k] for k in range(nb)]
        code = []
        for k in range(nb):
            rank = jnp.int32(0)
            for j in range(k):
                rank = rank + jnp.where(owners[j] == owners[k], 1, 0)
            code.append(owners[k] * ranks + rank)
        return code

    code = own_slots()

    to_after.wait_recv()
    to_before.wait_recv()
    to_after.wait_send()
    to_before.wait_send()
    is_first, is_last = me == 0, me == count - 1

    @pl.when(is_first)
    def _():
        outside = pl.ds(0, HALO * 8)
        fc[0, outside] = jnp.zeros((HALO * 8, 128), jnp.float32)
        fc[1, outside] = jnp.concatenate([fc[1, pl.ds(HALO * 8, 8)]] * HALO, axis=0)

    @pl.when(is_last)
    def _():
        outside = pl.ds((total + HALO) * 8, HALO * 8)
        fc[0, outside] = jnp.zeros((HALO * 8, 128), jnp.float32)
        fc[1, outside] = jnp.concatenate([fc[1, pl.ds((total + HALO - 1) * 8, 8)]] * HALO, axis=0)

    first(1, 2 + STEP)
    first(HALO + last * STEP, STEP + 2)

    def near(u, start, n):
        here = pl.ds(start, n)
        ax, ay = ax_s[here], ay_s[here]
        az = az_s[pl.ds(start - 1, n + 1)]
        mid = u[1:-1]
        return (
            ax * x_next(mid)
            + x_prev(ax * mid)
            + ay * y_next(mid)
            + y_prev(ay * mid)
            + az[1:] * u[2:]
            + az[:-1] * u[:-2]
        )

    def second(start, n):
        here = pl.ds(start, n)
        u = u1_s[pl.ds(start - 1, n + 2)]
        nu = near(u, start, n)
        u2 = (2.0 - WEIGHT) * u[1:-1] + inv_s[here] * nu
        u2_s[here] = u2
        return u2, nu

    def second_step(i, carry):
        start = HALO + i * STEP
        u2, nu = second(start, STEP)
        t_s[pl.ds(start, STEP)] = (1.0 - WEIGHT) ** 2 * field(0, start, STEP) - WEIGHT * nu
        per = layers // STEP
        inner = pl.ds(pl.multiple_of(lax.rem(i, per) * STEP * 8, STEP * 8), STEP * 8)
        boxes[i // per, inner] = u2.reshape(STEP * 8, 128).astype(jnp.bfloat16)
        return carry

    lax.fori_loop(0, total // STEP, second_step, 0, unroll=2)
    rows = layers * 8
    boxes[nb] = jnp.zeros((rows, 128), jnp.bfloat16)

    for d in range(n_grp):
        for r in range(ranks):
            pick = jnp.int32(nb)
            for k in range(nb):
                pick = jnp.where(code[k] == d * ranks + r, k, pick)
            slots[d, r] = boxes[pick]

    def corr_copy(off):
        to = lax.rem(me_g + off, n_grp)
        return pltpu.make_async_remote_copy(
            src_ref=slots.at[to],
            dst_ref=corr_ref.at[me_g],
            send_sem=corr_send.at[off],
            recv_sem=corr_recv.at[off],
            device_id=(me_s, to),
            device_id_type=MESH,
        )

    corr_own = pltpu.make_async_copy(slots.at[me_g], corr_ref.at[me_g], local_sem.at[0])

    def corr_start(off, carry):
        corr_copy(off).start()
        return carry

    lax.fori_loop(1, n_grp, corr_start, 0)
    corr_own.start()

    second(HALO - 1, 1)
    second(HALO + total, 1)

    @pl.when(is_first)
    def _():
        u2_s[pl.ds(HALO - 1, 1)] = jnp.zeros((1, 8, 128), jnp.float32)

    @pl.when(is_last)
    def _():
        u2_s[pl.ds(HALO + total, 1)] = jnp.zeros((1, 8, 128), jnp.float32)

    def residual_step(i, carry):
        start = HALO + i * STEP
        u = u2_s[pl.ds(start - 1, STEP + 2)]
        r = t_s[pl.ds(start, STEP)] + near(u, start, STEP)
        for j in range(STEP // 2):
            rs[i * (STEP // 2) + j] = r[2 * j] + r[2 * j + 1]
        return carry

    lax.fori_loop(0, total // STEP, residual_step, 0, unroll=2)

    cell = lax.broadcasted_iota(jnp.int32, (128, 128), 0)
    out = lax.broadcasted_iota(jnp.int32, (128, 128), 1)
    merge = jnp.where(out % 32 == (cell // 64) * 16 + (cell % 32) // 2, 0.125, 0.0).astype(
        jnp.bfloat16
    )
    half = layers // 2

    def restrict_step(k, carry):
        v = rs[pl.ds(k * half, half)].reshape(half * 8, 128)
        high = v.astype(jnp.bfloat16)
        rest = v - high.astype(jnp.float32)
        mid = rest.astype(jnp.bfloat16)
        low = (rest - mid.astype(jnp.float32)).astype(jnp.bfloat16)
        res[...] = (
            jnp.dot(low, merge, preferred_element_type=jnp.float32)
            + jnp.dot(mid, merge, preferred_element_type=jnp.float32)
            + jnp.dot(high, merge, preferred_element_type=jnp.float32)
        )
        lane = lax.broadcasted_iota(jnp.int32, (half * 2, 128), 1) // 32
        value = res[pl.ds(0, half * 2, stride=4), :]
        for p in range(1, 4):
            value = jnp.where(lane == p, res[pl.ds(p, half * 2, stride=4), :], value)
        coarse_s[pl.ds(pl.multiple_of(k * half * 2, half * 2), half * 2)] = value
        return carry

    lax.fori_loop(0, nb, restrict_step, 0)

    crow = nb * half * 2
    mine = pl.ds(pl.multiple_of(me_s * crow, crow), crow)

    def coarse_copy(off):
        return pltpu.make_async_remote_copy(
            src_ref=coarse_s,
            dst_ref=coarse_ref.at[mine],
            send_sem=coarse_send.at[off],
            recv_sem=coarse_recv.at[off],
            device_id=(lax.rem(me_s + off, n_box), me_g),
            device_id_type=MESH,
        )

    def coarse_start(off, carry):
        coarse_copy(off).start()
        return carry

    lax.fori_loop(1, n_box, coarse_start, 0)
    coarse_own = pltpu.make_async_copy(coarse_s, coarse_ref.at[mine], local_sem.at[1])
    coarse_own.start()

    def coarse_wait(off, carry):
        coarse_copy(off).wait()
        return carry

    def corr_wait(off, carry):
        corr_copy(off).wait()
        return carry

    lax.fori_loop(1, n_box, coarse_wait, 0)
    lax.fori_loop(1, n_grp, corr_wait, 0)
    corr_own.wait()
    coarse_own.wait()


def cells_major(field):
    return field.transpose(1, 2, 0).reshape(-1, field.shape[0])


def shards(source, conductivity, new_owner):
    total, rows_y, rows_x = source.shape
    nb = new_owner.shape[2]
    layers = total // nb
    n_box, n_grp = lax.axis_size("box"), lax.axis_size("grp")
    ranks = max(2, (2 * nb + n_grp - 1) // n_grp)
    rows = layers * 8
    deep = total + 2 * HALO
    plane = pltpu.VMEM((deep, 8, 128), jnp.float32)
    crow = total
    corr, coarse = pl.pallas_call(
        functools.partial(kernel, (n_box, n_grp, nb, layers, ranks)),
        out_shape=(
            jax.ShapeDtypeStruct((n_grp, ranks, rows, 128), jnp.bfloat16),
            jax.ShapeDtypeStruct((n_box * crow, 128), jnp.float32),
        ),
        in_specs=[
            pl.BlockSpec(memory_space=pltpu.SMEM),
            pl.BlockSpec(memory_space=pltpu.VMEM),
            pl.BlockSpec(memory_space=pltpu.VMEM),
        ],
        out_specs=[pl.BlockSpec(memory_space=pl.ANY)] * 2,
        scratch_shapes=[
            pltpu.VMEM((2, deep * 8, 128), jnp.float32),
            plane,
            plane,
            plane,
            plane,
            plane,
            plane,
            plane,
            pltpu.VMEM((nb + 1, rows, 128), jnp.bfloat16),
            pltpu.VMEM((n_grp, ranks, rows, 128), jnp.bfloat16),
            pltpu.VMEM((total // 2, 8, 128), jnp.float32),
            pltpu.VMEM((layers // 2 * 8, 128), jnp.float32),
            pltpu.VMEM((crow, 128), jnp.float32),
            pltpu.SemaphoreType.DMA((2,)),
            pltpu.SemaphoreType.DMA((2,)),
            pltpu.SemaphoreType.DMA((n_grp,)),
            pltpu.SemaphoreType.DMA((n_grp,)),
            pltpu.SemaphoreType.DMA((n_box,)),
            pltpu.SemaphoreType.DMA((n_box,)),
            pltpu.SemaphoreType.DMA((2,)),
        ],
        compiler_params=pltpu.CompilerParams(
            collective_id=0, has_side_effects=True, vmem_limit_bytes=40 * 1024 * 1024
        ),
        name="poisson",
    )(new_owner.reshape(nb), cells_major(source), cells_major(conductivity))
    return (
        corr.reshape(1, 1, n_grp, ranks, layers * rows_y * rows_x),
        coarse.reshape(1, n_box * nb, layers * rows_y * rows_x // 8),
    )


def solution(mesh):
    placed = (
        P(("box", "grp"), None, None),
        P(("box", "grp"), None, None),
        P("box", "grp", None, None),
    )
    return jax.shard_map(
        shards,
        mesh=mesh,
        in_specs=placed,
        out_specs=(P("box", "grp", None, None, None), P("grp", None, None)),
        check_vma=False,
    )
```

time: 128 us -> 33.2 us (0.26)
  blocking collectives: 36.9 us -> 0 us
  local copies, waits for them, and re-layouts: 37.8 us -> 4.88 us
  other arithmetic: 29.4 us -> 0 us
  Pallas kernels: 0 us -> 27.1 us
  between operations: 15 us -> 0.66 us
  starting transfers between devices: 6.29 us -> 0 us
  matrix products: 2.28 us -> 0 us
    pallas_call x0 -> x1, Pallas kernels: none -> 27.1 us  [shards(): pl.pallas_call(functools.partial(kernel, (n_box, n_grp, nb, layers, ranks...]
    unnamed x1 -> x0, blocking collectives: 24.7 us -> none
    another operation x1 -> x0, local copies, waits for them, and re-layouts: 23.9 us -> none  [restrict(): leftover.reshape(leading + (layers // 2, 2, rows_y // 2, 2, rows_x // 2, 2))]
    reduce_sum x2 -> x0, other arithmetic: 15.5 us -> none  [the longest x1 15.4 us: restrict(): return jnp.mean(blocks, axis=(-5, -3, -1)).reshape(leading + (-1,))]
    all_gather x1 -> x0, blocking collectives: 12.2 us -> none  [shards(): coarse = lax.all_gather(restricted, 'box', axis=0, tiled=True)]
    select_n x5 -> x0, other arithmetic: 6.5 us -> none  [the longest x1 2.26 us: smooth(): leftover = jnp.where(inside, source - operate(sweep_two), 0.0)]
    ppermute x2 -> x0, starting transfers between devices: 6.25 us -> none  [the longest x1 4.96 us: padded_2(): lax.ppermute(tail, axis, [(i, (i + 1) % count) for i in range(ends)])]
    unnamed x24 -> x6, local copies, waits for them, and re-layouts: 7.63 us -> 2.73 us
  transfers between devices with their start and end apart: 3 -> 0, of which waited for: 0 -> 0; matrix products, arithmetic and copies ran while one was open for 37% -> 0% of each run, Pallas kernels for 0% -> 0%
where the time goes in v1:
time: 33.2 us; the launch traced here: 32.6 us
  Pallas kernels  27.1 us (82%)
  local copies, waits for them, and re-layouts  4.88 us (15%)
  between operations  0.66 us (2%)
    pallas_call x1, Pallas kernels, shards(): pl.pallas_call(functools.partial(kernel, (n_box, n_grp, nb, layers, ranks...  27.1 us
    unnamed x6, local copies, waits for them, and re-layouts  2.73 us
    reshape x1, local copies, waits for them, and re-layouts, shards(): corr.reshape(1, 1, n_grp, ranks, layers * rows_y * rows_x)  1.14 us
    reshape x1, local copies, waits for them, and re-layouts, shards(): coarse.reshape(1, n_box * nb, layers * rows_y * rows_x // 8)  0.96 us

profile of v1, /device:TPU:0, one launch (start us, length us, event | category | flops | bytes accessed | tf_op | source)
XLA Modules:
  0.0 32.6 jit_solution(7787858126356421555)
XLA Ops:
  0.6 0.0 copy-start.2
  0.6 0.6 %copy-done.2 = s32[1,1,5,1]{2,3,1,0:T(1,128)S(1)} copy-done((s32[1,1,5,1]{2,3,1,0:T(1,128)S(1)}, s32[1,1,5,1]{2,3,1,0:T(1,128)}, u32[]{:S(2)}) %copy-start.2) | copy-done | bytes 44
  1.3 0.0 copy-start
  1.3 1.0 %copy-done = bf16[160,32,32]{0,2,1:T(8,128)(2,1)S(1)} copy-done((bf16[160,32,32]{0,2,1:T(8,128)(2,1)S(1)}, bf16[160,32,32]{0,2,1:T(8,128)(2,1)}, u32[]{:S(2)}) %copy-start) | copy-done | bytes 327704
  2.3 0.0 copy-start.1
  2.3 1.0 %copy-done.1 = bf16[160,32,32]{0,2,1:T(8,128)(2,1)S(1)} copy-done((bf16[160,32,32]{0,2,1:T(8,128)(2,1)S(1)}, bf16[160,32,32]{0,2,1:T(8,128)(2,1)}, u32[]{:S(2)}) %copy-start.1) | copy-done | bytes 327704
  3.4 27.1 %poisson.1 = (bf16[4,3,256,128]{3,2,1,0:T(8,128)(2,1)S(1)}, f32[1280,128]{1,0:T(8,128)S(1)}) custom-call(s32[5]{0:T(128)S(1)} %bitcast.13, bf16[1024,160]{1,0:T(8,128)(2,1)S(1)} %bitcast.11, bf16[1024,160]{1,0:T(8,128)(2,1)S(1)} %bitcast.12), custom_call_target="tpu_custom_call" | custom-call | tf_op jit(solution)/shard_map/poisson/pallas_call | solution.py:364
  30.5 0.1 copy.6
  30.5 1.1 %reshape.22 = bf16[1,1,4,3,32768]{4,2,3,1,0:T(4,128)(2,1)} reshape(bf16[4,3,256,128]{3,2,0,1:T(8,128)(2,1)S(1)} %copy.6) | data formatting | bytes 1572864 | tf_op jit(solution)/shard_map/reshape | solution.py:404
  31.7 1.0 %reshape.23 = f32[1,40,4096]{2,1,0:T(8,128)} reshape(f32[1280,128]{1,0:T(8,128)S(1)} %get-tuple-element.5) | data formatting | bytes 1310720 | tf_op jit(solution)/shard_map/reshape | solution.py:405
Async XLA Ops:
  0.6 0.7 %copy-start.2 = (s32[1,1,5,1]{2,3,1,0:T(1,128)S(1)}, s32[1,1,5,1]{2,3,1,0:T(1,128)}, u32[]{:S(2)}) copy-start(s32[1,1,5,1]{2,3,1,0:T(1,128)} %param.5) | copy-start | bytes 64
  1.3 1.0 %copy-start = (bf16[160,32,32]{0,2,1:T(8,128)(2,1)S(1)}, bf16[160,32,32]{0,2,1:T(8,128)(2,1)}, u32[]{:S(2)}) copy-start(bf16[160,32,32]{0,2,1:T(8,128)(2,1)} %param.3) | copy-start | bytes 983044
  2.3 1.0 %copy-start.1 = (bf16[160,32,32]{0,2,1:T(8,128)(2,1)S(1)}, bf16[160,32,32]{0,2,1:T(8,128)(2,1)}, u32[]{:S(2)}) copy-start(bf16[160,32,32]{0,2,1:T(8,128)(2,1)} %param.4) | copy-start | bytes 983044

commit v2 on v1

--- a/solution.py
+++ b/solution.py
@@ -9,6 +9,7 @@
 
 WEIGHT = 0.8
 HALO = 3
+EDGE = 2
 STEP = 8
 MESH = pl.DeviceIdType.MESH
 
@@ -41,11 +42,13 @@
 
 def kernel(
     sizes,
-    owner_ref,
-    source_ref,
-    cond_ref,
+    owner_hbm,
+    source_hbm,
+    cond_hbm,
     corr_ref,
     coarse_ref,
+    owner_ref,
+    field_s,
     fc,
     ax_s,
     ay_s,
@@ -66,6 +69,7 @@
     coarse_send,
     coarse_recv,
     local_sem,
+    input_sem,
 ):
     n_box, n_grp, nb, layers, ranks = sizes
     total = nb * layers
@@ -77,6 +81,21 @@
     after_id = (after // n_grp, lax.rem(after, n_grp))
     before_id = (before // n_grp, lax.rem(before, n_grp))
 
+    quarter = 8 * 32
+
+    def input_copy(which, b):
+        part = pl.ds(b * quarter, quarter)
+        ref = (source_hbm, cond_hbm)[which]
+        return pltpu.make_async_copy(
+            ref.at[part], field_s.at[which, part], input_sem.at[which * 4 + b]
+        )
+
+    owner_copy = pltpu.make_async_copy(owner_hbm, owner_ref, input_sem.at[8])
+    for which in (1, 0):
+        for b in range(4):
+            input_copy(which, b).start()
+    owner_copy.start()
+
     barrier = pltpu.get_barrier_semaphore()
     for target in (after_id, before_id):
         pl.semaphore_signal(barrier, inc=1, device_id=target, device_id_type=MESH)
@@ -100,11 +119,12 @@
         1.0,
         0.0,
     ).astype(jnp.bfloat16)
-    for which, ref in enumerate((source_ref, cond_ref)):
+    for which in (1, 0):
         for b in range(4):
+            input_copy(which, b).wait()
             turned = lax.dot_general(
                 eye,
-                ref[pl.ds(b * 256, 256)],
+                field_s[which, pl.ds(b * quarter, quarter)],
                 (((1,), (1,)), ((), ())),
                 preferred_element_type=jnp.float32,
             )
@@ -167,40 +187,10 @@
         return carry
 
     last = total // STEP - 1
+    tail = HALO + last * STEP
+    first(HALO + 1, STEP - 1)
     lax.fori_loop(1, last, first_step, 0, unroll=2)
-
-    def own_slots():
-        owners = [owner_ref[k] for k in range(nb)]
-        code = []
-        for k in range(nb):
-            rank = jnp.int32(0)
-            for j in range(k):
-                rank = rank + jnp.where(owners[j] == owners[k], 1, 0)
-            code.append(owners[k] * ranks + rank)
-        return code
-
-    code = own_slots()
-
-    to_after.wait_recv()
-    to_before.wait_recv()
-    to_after.wait_send()
-    to_before.wait_send()
-    is_first, is_last = me == 0, me == count - 1
-
-    @pl.when(is_first)
-    def _():
-        outside = pl.ds(0, HALO * 8)
-        fc[0, outside] = jnp.zeros((HALO * 8, 128), jnp.float32)
-        fc[1, outside] = jnp.concatenate([fc[1, pl.ds(HALO * 8, 8)]] * HALO, axis=0)
-
-    @pl.when(is_last)
-    def _():
-        outside = pl.ds((total + HALO) * 8, HALO * 8)
-        fc[0, outside] = jnp.zeros((HALO * 8, 128), jnp.float32)
-        fc[1, outside] = jnp.concatenate([fc[1, pl.ds((total + HALO - 1) * 8, 8)]] * HALO, axis=0)
-
-    first(1, 2 + STEP)
-    first(HALO + last * STEP, STEP + 2)
+    first(tail, STEP - 1)
 
     def near(u, start, n):
         here = pl.ds(start, n)
@@ -224,48 +214,103 @@
         u2_s[here] = u2
         return u2, nu
 
+    rows = layers * 8
+
+    def settle(start, n):
+        u2, nu = second(start, n)
+        t_s[pl.ds(start, n)] = (1.0 - WEIGHT) ** 2 * field(0, start, n) - WEIGHT * nu
+        return u2.reshape(n * 8, 128).astype(jnp.bfloat16)
+
     def second_step(i, carry):
-        start = HALO + i * STEP
-        u2, nu = second(start, STEP)
-        t_s[pl.ds(start, STEP)] = (1.0 - WEIGHT) ** 2 * field(0, start, STEP) - WEIGHT * nu
         per = layers // STEP
         inner = pl.ds(pl.multiple_of(lax.rem(i, per) * STEP * 8, STEP * 8), STEP * 8)
-        boxes[i // per, inner] = u2.reshape(STEP * 8, 128).astype(jnp.bfloat16)
-        return carry
-
-    lax.fori_loop(0, total // STEP, second_step, 0, unroll=2)
-    rows = layers * 8
+        boxes[i // per, inner] = settle(HALO + i * STEP, STEP)
+        return carry
+
+    edge = EDGE * 8
+    inner_rows = (STEP - EDGE) * 8
+    boxes[0, pl.ds(edge, inner_rows)] = settle(HALO + EDGE, STEP - EDGE)
+    lax.fori_loop(1, last, second_step, 0, unroll=2)
+    boxes[nb - 1, pl.ds(rows - STEP * 8, inner_rows)] = settle(tail, STEP - EDGE)
     boxes[nb] = jnp.zeros((rows, 128), jnp.bfloat16)
 
-    for d in range(n_grp):
-        for r in range(ranks):
-            pick = jnp.int32(nb)
-            for k in range(nb):
-                pick = jnp.where(code[k] == d * ranks + r, k, pick)
-            slots[d, r] = boxes[pick]
-
-    def corr_copy(off):
+    owner_copy.wait()
+    def own_slots():
+        owners = [owner_ref[k] for k in range(nb)]
+        code = []
+        for k in range(nb):
+            rank = jnp.int32(0)
+            for j in range(k):
+                rank = rank + jnp.where(owners[j] == owners[k], 1, 0)
+            code.append(owners[k] * ranks + rank)
+        return code
+
+    code = own_slots()
+    picks = []
+    for j in range(n_grp * ranks):
+        pick = jnp.int32(nb)
+        for k in range(nb):
+            pick = jnp.where(code[k] == j, k, pick)
+        picks.append(pick)
+
+    pieces = (pl.ds(edge, rows - 2 * edge), pl.ds(0, edge), pl.ds(rows - edge, edge))
+
+    def fill(piece):
+        for j in range(n_grp * ranks):
+            slots[j // ranks, j % ranks, piece] = boxes[picks[j], piece]
+
+    def corr_copy(off, p):
         to = lax.rem(me_g + off, n_grp)
         return pltpu.make_async_remote_copy(
-            src_ref=slots.at[to],
-            dst_ref=corr_ref.at[me_g],
-            send_sem=corr_send.at[off],
-            recv_sem=corr_recv.at[off],
+            src_ref=slots.at[to, :, pieces[p]],
+            dst_ref=corr_ref.at[me_g, :, pieces[p]],
+            send_sem=corr_send.at[off * 3 + p],
+            recv_sem=corr_recv.at[off * 3 + p],
             device_id=(me_s, to),
             device_id_type=MESH,
         )
 
+    fill(pieces[0])
+
+    def main_start(off, carry):
+        corr_copy(off, 0).start()
+        return carry
+
+    lax.fori_loop(1, n_grp, main_start, 0)
+
+    to_after.wait_recv()
+    to_before.wait_recv()
+    to_after.wait_send()
+    to_before.wait_send()
+    is_first, is_last = me == 0, me == count - 1
+
+    @pl.when(is_first)
+    def _():
+        outside = pl.ds(0, HALO * 8)
+        fc[0, outside] = jnp.zeros((HALO * 8, 128), jnp.float32)
+        fc[1, outside] = jnp.concatenate([fc[1, pl.ds(HALO * 8, 8)]] * HALO, axis=0)
+
+    @pl.when(is_last)
+    def _():
+        outside = pl.ds((total + HALO) * 8, HALO * 8)
+        fc[0, outside] = jnp.zeros((HALO * 8, 128), jnp.float32)
+        fc[1, outside] = jnp.concatenate([fc[1, pl.ds((total + HALO - 1) * 8, 8)]] * HALO, axis=0)
+
+    first(1, HALO)
+    first(HALO + total - 1, HALO)
+    boxes[0, pl.ds(0, edge)] = settle(HALO - 1, EDGE + 1)[8:]
+    boxes[nb - 1, pl.ds(rows - edge, edge)] = settle(HALO + total - EDGE, EDGE + 1)[:-8]
+    fill(pieces[1])
+    fill(pieces[2])
+
+    def edge_start(off, carry):
+        corr_copy(off, 1).start()
+        corr_copy(off, 2).start()
+        return carry
+
+    lax.fori_loop(1, n_grp, edge_start, 0)
     corr_own = pltpu.make_async_copy(slots.at[me_g], corr_ref.at[me_g], local_sem.at[0])
-
-    def corr_start(off, carry):
-        corr_copy(off).start()
-        return carry
-
-    lax.fori_loop(1, n_grp, corr_start, 0)
     corr_own.start()
-
-    second(HALO - 1, 1)
-    second(HALO + total, 1)
 
     @pl.when(is_first)
     def _():
@@ -338,7 +383,8 @@
         return carry
 
     def corr_wait(off, carry):
-        corr_copy(off).wait()
+        for p in range(3):
+            corr_copy(off, p).wait()
         return carry
 
     lax.fori_loop(1, n_box, coarse_wait, 0)
@@ -368,12 +414,14 @@
             jax.ShapeDtypeStruct((n_box * crow, 128), jnp.float32),
         ),
         in_specs=[
-            pl.BlockSpec(memory_space=pltpu.SMEM),
-            pl.BlockSpec(memory_space=pltpu.VMEM),
-            pl.BlockSpec(memory_space=pltpu.VMEM),
+            pl.BlockSpec(memory_space=pltpu.HBM),
+            pl.BlockSpec(memory_space=pltpu.HBM),
+            pl.BlockSpec(memory_space=pltpu.HBM),
         ],
         out_specs=[pl.BlockSpec(memory_space=pl.ANY)] * 2,
         scratch_shapes=[
+            pltpu.SMEM((nb,), jnp.int32),
+            pltpu.VMEM((2, rows_y * rows_x, total), jnp.bfloat16),
             pltpu.VMEM((2, deep * 8, 128), jnp.float32),
             plane,
             plane,
@@ -389,14 +437,15 @@
             pltpu.VMEM((crow, 128), jnp.float32),
             pltpu.SemaphoreType.DMA((2,)),
             pltpu.SemaphoreType.DMA((2,)),
-            pltpu.SemaphoreType.DMA((n_grp,)),
-            pltpu.SemaphoreType.DMA((n_grp,)),
+            pltpu.SemaphoreType.DMA((n_grp * 3,)),
+            pltpu.SemaphoreType.DMA((n_grp * 3,)),
             pltpu.SemaphoreType.DMA((n_box,)),
             pltpu.SemaphoreType.DMA((n_box,)),
             pltpu.SemaphoreType.DMA((2,)),
+            pltpu.SemaphoreType.DMA((9,)),
         ],
         compiler_params=pltpu.CompilerParams(
-            collective_id=0, has_side_effects=True, vmem_limit_bytes=40 * 1024 * 1024
+            collective_id=0, has_side_effects=True, vmem_limit_bytes=62 * 1024 * 1024
         ),
         name="poisson",
     )(new_owner.reshape(nb), cells_major(source), cells_major(conductivity))

time: 33.2 us -> 32.7 us (0.985); the launches traced: 32.6 us -> 32.5 us
  local copies, waits for them, and re-layouts: 4.88 us -> 3.29 us
  Pallas kernels: 27.1 us -> 28.6 us
    unnamed x6 -> x2, local copies, waits for them, and re-layouts: 2.73 us -> 0.01 us
    pallas_call x1, Pallas kernels: 27.1 us -> 28.6 us  [shards(): pl.pallas_call(functools.partial(kernel, (n_box, n_grp, nb, layers, ranks...]
    pallas_call x1, local copies, waits for them, and re-layouts: 0.05 us -> 1.19 us  [shards(): pl.pallas_call(functools.partial(kernel, (n_box, n_grp, nb, layers, ranks...]
where the time goes in v2:
time: 32.7 us; the launch traced here: 32.5 us
  Pallas kernels  28.6 us (87%)
  local copies, waits for them, and re-layouts  3.29 us (10%)
  between operations  0.65 us (2%)
    pallas_call x1, Pallas kernels, shards(): pl.pallas_call(functools.partial(kernel, (n_box, n_grp, nb, layers, ranks...  28.6 us
    pallas_call x1, local copies, waits for them, and re-layouts, shards(): pl.pallas_call(functools.partial(kernel, (n_box, n_grp, nb, layers, ranks...  1.19 us
    reshape x1, local copies, waits for them, and re-layouts, shards(): corr.reshape(1, 1, n_grp, ranks, layers * rows_y * rows_x)  1.14 us
    reshape x1, local copies, waits for them, and re-layouts, shards(): coarse.reshape(1, n_box * nb, layers * rows_y * rows_x // 8)  0.96 us

profile of v2, /device:TPU:0, one launch (start us, length us, event | category | flops | bytes accessed | tf_op | source)
XLA Modules:
  0.0 32.5 jit_solution(5379939085563122495)
XLA Ops:
  0.6 28.6 %poisson.1 = (bf16[4,3,256,128]{3,2,1,0:T(8,128)(2,1)}, f32[1280,128]{1,0:T(8,128)}) custom-call(s32[5]{0:T(128)} %bitcast.13, bf16[1024,160]{1,0:T(8,128)(2,1)} %bitcast.11, bf16[1024,160]{1,0:T(8,128)(2,1)} %bitcast.12), custom_call_target="tpu_custom_call" | custom-call | tf_op jit(solution)/shard_map/poisson/pallas_call | solution.py:410
  29.2 1.2 %copy.6 = bf16[4,3,256,128]{3,2,0,1:T(8,128)(2,1)S(1)} copy(bf16[4,3,256,128]{3,2,1,0:T(8,128)(2,1)} %get-tuple-element.4) | data formatting | bytes 1572864 | tf_op jit(solution)/shard_map/poisson/pallas_call | solution.py:410
  30.4 0.0 copy-start
  30.4 1.1 %reshape.22 = bf16[1,1,4,3,32768]{4,2,3,1,0:T(4,128)(2,1)} reshape(bf16[4,3,256,128]{3,2,0,1:T(8,128)(2,1)S(1)} %copy.6) | data formatting | bytes 1572864 | tf_op jit(solution)/shard_map/reshape | solution.py:453
  31.6 0.0 copy-done
  31.6 1.0 %reshape.23 = f32[1,40,4096]{2,1,0:T(8,128)} reshape(f32[1280,128]{1,0:T(8,128)S(1)} %copy-done) | data formatting | bytes 1310720 | tf_op jit(solution)/shard_map/reshape | solution.py:454
Async XLA Ops:
  30.4 1.2 %copy-start = (f32[1280,128]{1,0:T(8,128)S(1)}, f32[1280,128]{1,0:T(8,128)}, u32[]{:S(2)}) copy-start(f32[1280,128]{1,0:T(8,128)} %get-tuple-element.5) | copy-start | bytes 1966084

commit v3 on v2

--- a/solution.py
+++ b/solution.py
@@ -70,8 +70,19 @@
     coarse_recv,
     local_sem,
     input_sem,
+    xs,
+    xin,
+    xout,
+    flags,
+    flags_in,
+    x_send,
+    x_recv,
+    f_send,
+    flag_send,
+    flag_recv,
 ):
     n_box, n_grp, nb, layers, ranks = sizes
+    shared = n_grp == 4 and nb < 2 * ranks
     total = nb * layers
     me_s, me_g = lax.axis_index("box"), lax.axis_index("grp")
     me = me_s * n_grp + me_g
@@ -189,7 +200,7 @@
     last = total // STEP - 1
     tail = HALO + last * STEP
     first(HALO + 1, STEP - 1)
-    lax.fori_loop(1, last, first_step, 0, unroll=2)
+    lax.fori_loop(1, last, first_step, 0, unroll=6)
     first(tail, STEP - 1)
 
     def near(u, start, n):
@@ -230,7 +241,7 @@
     edge = EDGE * 8
     inner_rows = (STEP - EDGE) * 8
     boxes[0, pl.ds(edge, inner_rows)] = settle(HALO + EDGE, STEP - EDGE)
-    lax.fori_loop(1, last, second_step, 0, unroll=2)
+    lax.fori_loop(1, last, second_step, 0, unroll=6)
     boxes[nb - 1, pl.ds(rows - STEP * 8, inner_rows)] = settle(tail, STEP - EDGE)
     boxes[nb] = jnp.zeros((rows, 128), jnp.bfloat16)
 
@@ -253,30 +264,66 @@
             pick = jnp.where(code[k] == j, k, pick)
         picks.append(pick)
 
-    pieces = (pl.ds(edge, rows - 2 * edge), pl.ds(0, edge), pl.ds(rows - edge, edge))
-
-    def fill(piece):
-        for j in range(n_grp * ranks):
-            slots[j // ranks, j % ranks, piece] = boxes[picks[j], piece]
-
-    def corr_copy(off, p):
-        to = lax.rem(me_g + off, n_grp)
+    inner, head, foot = (
+        pl.ds(edge, rows - 2 * edge),
+        pl.ds(0, edge),
+        pl.ds(rows - edge, edge),
+    )
+
+    half_g = me_g // 2
+    partner = me_g + 1 - 2 * lax.rem(me_g, 2)
+    near_g, far_g = 2 - half_g, 3 - 3 * half_g
+    across = 2 - 2 * half_g
+    is_near = me_g == 1 + half_g
+
+    def shared_copy(piece, p):
         return pltpu.make_async_remote_copy(
-            src_ref=slots.at[to, :, pieces[p]],
-            dst_ref=corr_ref.at[me_g, :, pieces[p]],
-            send_sem=corr_send.at[off * 3 + p],
-            recv_sem=corr_recv.at[off * 3 + p],
+            src_ref=xs.at[piece],
+            dst_ref=xin.at[lax.rem(me_g, 2), piece],
+            send_sem=x_send.at[p],
+            recv_sem=x_recv.at[lax.rem(me_g, 2) * 3 + p],
+            device_id=(me_s, near_g),
+            device_id_type=MESH,
+        )
+
+    def forward_copy(k, piece, p):
+        return pltpu.make_async_remote_copy(
+            src_ref=xin.at[k, piece],
+            dst_ref=xin.at[k, piece],
+            send_sem=f_send.at[k * 3 + p],
+            recv_sem=x_recv.at[k * 3 + p],
+            device_id=(me_s, partner),
+            device_id_type=MESH,
+        )
+
+    def flag_copy(to, p):
+        return pltpu.make_async_remote_copy(
+            src_ref=flags.at[to],
+            dst_ref=flags_in.at[me_g],
+            send_sem=flag_send.at[p],
+            recv_sem=flag_recv.at[me_g],
             device_id=(me_s, to),
             device_id_type=MESH,
         )
 
-    fill(pieces[0])
-
-    def main_start(off, carry):
-        corr_copy(off, 0).start()
-        return carry
-
-    lax.fori_loop(1, n_grp, main_start, 0)
+    def corr_copy(to, sender, count, p):
+        return pltpu.make_async_remote_copy(
+            src_ref=slots.at[pl.ds(0, count), to],
+            dst_ref=corr_ref.at[pl.ds(0, count), sender],
+            send_sem=corr_send.at[p],
+            recv_sem=corr_recv.at[sender],
+            device_id=(me_s, to),
+            device_id_type=MESH,
+        )
+
+    if shared:
+        lows = [jnp.minimum(picks[2 * h * ranks + ranks - 1], picks[(2 * h + 1) * ranks + ranks - 1]) for h in range(2)]
+        pick_x = jnp.where(half_g == 0, lows[1], lows[0])
+        xs[inner] = boxes[pick_x, inner]
+        shared_copy(inner, 0).start()
+        for d in range(n_grp):
+            flag = jnp.where(picks[d * ranks + ranks - 1] < nb, 1.0, 0.0)
+            flags[d] = jnp.full((16, 128), flag, jnp.float32).astype(jnp.bfloat16)
 
     to_after.wait_recv()
     to_before.wait_recv()
@@ -300,16 +347,27 @@
     first(HALO + total - 1, HALO)
     boxes[0, pl.ds(0, edge)] = settle(HALO - 1, EDGE + 1)[8:]
     boxes[nb - 1, pl.ds(rows - edge, edge)] = settle(HALO + total - EDGE, EDGE + 1)[:-8]
-    fill(pieces[1])
-    fill(pieces[2])
-
-    def edge_start(off, carry):
-        corr_copy(off, 1).start()
-        corr_copy(off, 2).start()
-        return carry
-
-    lax.fori_loop(1, n_grp, edge_start, 0)
-    corr_own = pltpu.make_async_copy(slots.at[me_g], corr_ref.at[me_g], local_sem.at[0])
+    if shared:
+        xs[head] = boxes[pick_x, head]
+        xs[foot] = boxes[pick_x, foot]
+        shared_copy(head, 1).start()
+        shared_copy(foot, 2).start()
+    for j in range(n_grp * ranks):
+        slots[j % ranks, j // ranks] = boxes[picks[j]]
+    if shared:
+        corr_copy(far_g, me_g, ranks - 1, 0).start()
+        corr_copy(near_g, me_g, ranks - 1, 1).start()
+        corr_copy(partner, me_g, ranks, 2).start()
+        flag_copy(near_g, 0).start()
+        flag_copy(far_g, 1).start()
+    else:
+
+        def corr_start(off, carry):
+            corr_copy(lax.rem(me_g + off, n_grp), me_g, ranks, off).start()
+            return carry
+
+        lax.fori_loop(1, n_grp, corr_start, 0)
+    corr_own = pltpu.make_async_copy(slots.at[:, me_g], corr_ref.at[:, me_g], local_sem.at[0])
     corr_own.start()
 
     @pl.when(is_first)
@@ -328,7 +386,7 @@
             rs[i * (STEP // 2) + j] = r[2 * j] + r[2 * j + 1]
         return carry
 
-    lax.fori_loop(0, total // STEP, residual_step, 0, unroll=2)
+    lax.fori_loop(0, total // STEP, residual_step, 0, unroll=5)
 
     cell = lax.broadcasted_iota(jnp.int32, (128, 128), 0)
     out = lax.broadcasted_iota(jnp.int32, (128, 128), 1)
@@ -382,13 +440,64 @@
         coarse_copy(off).wait()
         return carry
 
-    def corr_wait(off, carry):
+    if shared:
+        whole = (inner, head, foot)
+        for k in range(2):
+            for p in range(3):
+                forward_copy(k, whole[p], p).wait_recv()
+
+            @pl.when(is_near)
+            def _():
+                for p in range(3):
+                    forward_copy(k, whole[p], p).start()
+
+        for k in range(2):
+            flag_copy_in = pltpu.make_async_remote_copy(
+                src_ref=flags.at[0],
+                dst_ref=flags_in.at[across + k],
+                send_sem=flag_send.at[0],
+                recv_sem=flag_recv.at[across + k],
+                device_id=(me_s, partner),
+                device_id_type=MESH,
+            )
+            flag_copy_in.wait_recv()
+            kept = xin[k].reshape(rows // 16, 16, 128) * flags_in[across + k][None]
+            xout[k] = kept.reshape(rows, 128)
+            pltpu.make_async_copy(
+                xout.at[k], corr_ref.at[ranks - 1, across + k], local_sem.at[2 + k]
+            ).start()
+
+    lax.fori_loop(1, n_box, coarse_wait, 0)
+    if shared:
+        for k in range(2):
+            pltpu.make_async_copy(
+                xout.at[k], corr_ref.at[ranks - 1, across + k], local_sem.at[2 + k]
+            ).wait()
+            corr_copy(partner, across + k, ranks - 1, 0).wait_recv()
+        corr_copy(partner, partner, ranks, 2).wait_recv()
+        corr_copy(far_g, me_g, ranks - 1, 0).wait_send()
+        corr_copy(near_g, me_g, ranks - 1, 1).wait_send()
+        corr_copy(partner, me_g, ranks, 2).wait_send()
+        flag_copy(near_g, 0).wait_send()
+        flag_copy(far_g, 1).wait_send()
         for p in range(3):
-            corr_copy(off, p).wait()
-        return carry
-
-    lax.fori_loop(1, n_box, coarse_wait, 0)
-    lax.fori_loop(1, n_grp, corr_wait, 0)
+            shared_copy(whole[p], p).wait_send()
+
+        @pl.when(is_near)
+        def _():
+            for k in range(2):
+                for p in range(3):
+                    forward_copy(k, whole[p], p).wait_send()
+
+    else:
+
+        def corr_wait(off, carry):
+            corr_copy(lax.rem(me_g + off, n_grp), me_g, ranks, off).wait_send()
+            sender = lax.rem(me_g + off, n_grp)
+            corr_copy(sender, sender, ranks, off).wait_recv()
+            return carry
+
+        lax.fori_loop(1, n_grp, corr_wait, 0)
     corr_own.wait()
     coarse_own.wait()
 
@@ -410,7 +519,7 @@
     corr, coarse = pl.pallas_call(
         functools.partial(kernel, (n_box, n_grp, nb, layers, ranks)),
         out_shape=(
-            jax.ShapeDtypeStruct((n_grp, ranks, rows, 128), jnp.bfloat16),
+            jax.ShapeDtypeStruct((ranks, n_grp, rows, 128), jnp.bfloat16),
             jax.ShapeDtypeStruct((n_box * crow, 128), jnp.float32),
         ),
         in_specs=[
@@ -431,18 +540,28 @@
             plane,
             plane,
             pltpu.VMEM((nb + 1, rows, 128), jnp.bfloat16),
-            pltpu.VMEM((n_grp, ranks, rows, 128), jnp.bfloat16),
+            pltpu.VMEM((ranks, n_grp, rows, 128), jnp.bfloat16),
             pltpu.VMEM((total // 2, 8, 128), jnp.float32),
             pltpu.VMEM((layers // 2 * 8, 128), jnp.float32),
             pltpu.VMEM((crow, 128), jnp.float32),
             pltpu.SemaphoreType.DMA((2,)),
             pltpu.SemaphoreType.DMA((2,)),
-            pltpu.SemaphoreType.DMA((n_grp * 3,)),
-            pltpu.SemaphoreType.DMA((n_grp * 3,)),
+            pltpu.SemaphoreType.DMA((n_grp,)),
+            pltpu.SemaphoreType.DMA((n_grp,)),
             pltpu.SemaphoreType.DMA((n_box,)),
             pltpu.SemaphoreType.DMA((n_box,)),
+            pltpu.SemaphoreType.DMA((4,)),
+            pltpu.SemaphoreType.DMA((9,)),
+            pltpu.VMEM((rows, 128), jnp.bfloat16),
+            pltpu.VMEM((2, rows, 128), jnp.bfloat16),
+            pltpu.VMEM((2, rows, 128), jnp.bfloat16),
+            pltpu.VMEM((n_grp, 16, 128), jnp.bfloat16),
+            pltpu.VMEM((n_grp, 16, 128), jnp.bfloat16),
+            pltpu.SemaphoreType.DMA((3,)),
+            pltpu.SemaphoreType.DMA((6,)),
+            pltpu.SemaphoreType.DMA((6,)),
             pltpu.SemaphoreType.DMA((2,)),
-            pltpu.SemaphoreType.DMA((9,)),
+            pltpu.SemaphoreType.DMA((n_grp,)),
         ],
         compiler_params=pltpu.CompilerParams(
             collective_id=0, has_side_effects=True, vmem_limit_bytes=62 * 1024 * 1024
@@ -450,7 +569,7 @@
         name="poisson",
     )(new_owner.reshape(nb), cells_major(source), cells_major(conductivity))
     return (
-        corr.reshape(1, 1, n_grp, ranks, layers * rows_y * rows_x),
+        corr.reshape(ranks, n_grp, rows * 128).transpose(1, 0, 2)[None, None],
         coarse.reshape(1, n_box * nb, layers * rows_y * rows_x // 8),
     )
 

time: 32.7 us -> 30.3 us (0.927)
  Pallas kernels: 28.6 us -> 25.9 us
    pallas_call x1, Pallas kernels: 28.6 us -> 25.9 us  [shards(): pl.pallas_call(functools.partial(kernel, (n_box, n_grp, nb, layers, ranks...]
    reshape x1, local copies, waits for them, and re-layouts: 1.14 us -> 2.63 us  [shards(): corr.reshape(ranks, n_grp, rows * 128).transpose(1, 0, 2)[None, None]]
    pallas_call x1 -> x0, local copies, waits for them, and re-layouts: 1.19 us -> none  [shards(): pl.pallas_call(functools.partial(kernel, (n_box, n_grp, nb, layers, ranks...]
where the time goes in v3:
time: 30.3 us; the launch traced here: 30.2 us
  Pallas kernels  25.9 us (85%)
  local copies, waits for them, and re-layouts  3.59 us (12%)
  between operations  0.65 us (2%)
    pallas_call x1, Pallas kernels, shards(): pl.pallas_call(functools.partial(kernel, (n_box, n_grp, nb, layers, ranks...  25.9 us
    reshape x1, local copies, waits for them, and re-layouts, shards(): corr.reshape(ranks, n_grp, rows * 128).transpose(1, 0, 2)[None, None]  2.63 us
    reshape x1, local copies, waits for them, and re-layouts, shards(): coarse.reshape(1, n_box * nb, layers * rows_y * rows_x // 8)  0.96 us

profile of v3, /device:TPU:0, one launch (start us, length us, event | category | flops | bytes accessed | tf_op | source)
XLA Modules:
  0.0 30.2 jit_solution(1873062490002000022)
XLA Ops:
  0.6 25.9 %poisson.1 = (bf16[3,4,256,128]{3,2,1,0:T(8,128)(2,1)}, f32[1280,128]{1,0:T(8,128)}) custom-call(s32[5]{0:T(128)} %bitcast.15, bf16[1024,160]{1,0:T(8,128)(2,1)} %bitcast.13, bf16[1024,160]{1,0:T(8,128)(2,1)} %bitcast.14), custom_call_target="tpu_custom_call" | custom-call | tf_op jit(solution)/shard_map/poisson/pallas_call | solution.py:519
  26.6 0.0 copy-start
  26.6 2.6 %reshape.22 = bf16[3,4,32768]{2,1,0:T(4,128)(2,1)} reshape(bf16[3,4,256,128]{3,2,1,0:T(8,128)(2,1)} %get-tuple-element.4) | data formatting | bytes 1572864 | tf_op jit(solution)/shard_map/reshape | solution.py:572
  29.2 0.0 copy-done
  29.2 1.0 %reshape.23 = f32[1,40,4096]{2,1,0:T(8,128)} reshape(f32[1280,128]{1,0:T(8,128)S(1)} %copy-done) | data formatting | bytes 1310720 | tf_op jit(solution)/shard_map/reshape | solution.py:573
Async XLA Ops:
  26.6 2.6 %copy-start = (f32[1280,128]{1,0:T(8,128)S(1)}, f32[1280,128]{1,0:T(8,128)}, u32[]{:S(2)}) copy-start(f32[1280,128]{1,0:T(8,128)} %get-tuple-element.5) | copy-start | bytes 1966084

commit v4 on v3

--- a/solution.py
+++ b/solution.py
@@ -80,6 +80,8 @@
     f_send,
     flag_send,
     flag_recv,
+    far_send,
+    far_recv,
 ):
     n_box, n_grp, nb, layers, ranks = sizes
     shared = n_grp == 4 and nb < 2 * ranks
@@ -306,6 +308,22 @@
             device_id_type=MESH,
         )
 
+    whole = (inner, head, foot)
+
+    def far_copy(to, sender, p):
+        return pltpu.make_async_remote_copy(
+            src_ref=slots.at[pl.ds(0, ranks - 1), to, whole[p]],
+            dst_ref=corr_ref.at[pl.ds(0, ranks - 1), sender, whole[p]],
+            send_sem=far_send.at[p],
+            recv_sem=far_recv.at[lax.rem(sender, 2) * 3 + p],
+            device_id=(me_s, to),
+            device_id_type=MESH,
+        )
+
+    def fill(part):
+        for j in range(n_grp * ranks):
+            slots[j % ranks, j // ranks, part] = boxes[picks[j], part]
+
     def corr_copy(to, sender, count, p):
         return pltpu.make_async_remote_copy(
             src_ref=slots.at[pl.ds(0, count), to],
@@ -321,6 +339,9 @@
         pick_x = jnp.where(half_g == 0, lows[1], lows[0])
         xs[inner] = boxes[pick_x, inner]
         shared_copy(inner, 0).start()
+    fill(inner)
+    if shared:
+        far_copy(far_g, me_g, 0).start()
         for d in range(n_grp):
             flag = jnp.where(picks[d * ranks + ranks - 1] < nb, 1.0, 0.0)
             flags[d] = jnp.full((16, 128), flag, jnp.float32).astype(jnp.bfloat16)
@@ -352,10 +373,11 @@
         xs[foot] = boxes[pick_x, foot]
         shared_copy(head, 1).start()
         shared_copy(foot, 2).start()
-    for j in range(n_grp * ranks):
-        slots[j % ranks, j // ranks] = boxes[picks[j]]
+    fill(head)
+    fill(foot)
     if shared:
-        corr_copy(far_g, me_g, ranks - 1, 0).start()
+        far_copy(far_g, me_g, 1).start()
+        far_copy(far_g, me_g, 2).start()
         corr_copy(near_g, me_g, ranks - 1, 1).start()
         corr_copy(partner, me_g, ranks, 2).start()
         flag_copy(near_g, 0).start()
@@ -441,14 +463,12 @@
         return carry
 
     if shared:
-        whole = (inner, head, foot)
-        for k in range(2):
-            for p in range(3):
+        for p in range(3):
+            for k in range(2):
                 forward_copy(k, whole[p], p).wait_recv()
 
-            @pl.when(is_near)
-            def _():
-                for p in range(3):
+                @pl.when(is_near)
+                def _():
                     forward_copy(k, whole[p], p).start()
 
         for k in range(2):
@@ -473,9 +493,19 @@
             pltpu.make_async_copy(
                 xout.at[k], corr_ref.at[ranks - 1, across + k], local_sem.at[2 + k]
             ).wait()
-            corr_copy(partner, across + k, ranks - 1, 0).wait_recv()
+
+            @pl.when(is_near)
+            def _():
+                corr_copy(partner, across + k, ranks - 1, 0).wait_recv()
+
+            @pl.when(jnp.logical_not(is_near))
+            def _():
+                for p in range(3):
+                    far_copy(partner, across + k, p).wait_recv()
+
         corr_copy(partner, partner, ranks, 2).wait_recv()
-        corr_copy(far_g, me_g, ranks - 1, 0).wait_send()
+        for p in range(3):
+            far_copy(far_g, me_g, p).wait_send()
         corr_copy(near_g, me_g, ranks - 1, 1).wait_send()
         corr_copy(partner, me_g, ranks, 2).wait_send()
         flag_copy(near_g, 0).wait_send()
@@ -562,6 +592,8 @@
             pltpu.SemaphoreType.DMA((6,)),
             pltpu.SemaphoreType.DMA((2,)),
             pltpu.SemaphoreType.DMA((n_grp,)),
+            pltpu.SemaphoreType.DMA((3,)),
+            pltpu.SemaphoreType.DMA((6,)),
         ],
         compiler_params=pltpu.CompilerParams(
             collective_id=0, has_side_effects=True, vmem_limit_bytes=62 * 1024 * 1024

time: 30.3 us -> 30.4 us (level)
  no operation moved by 1% of the time
where the time goes in v4:
time: 30.4 us; the launch traced here: 30.2 us
  Pallas kernels  26 us (86%)
  local copies, waits for them, and re-layouts  3.59 us (12%)
  between operations  0.65 us (2%)
    pallas_call x1, Pallas kernels, shards(): pl.pallas_call(functools.partial(kernel, (n_box, n_grp, nb, layers, ranks...  26 us
    reshape x1, local copies, waits for them, and re-layouts, shards(): corr.reshape(ranks, n_grp, rows * 128).transpose(1, 0, 2)[None, None]  2.63 us
    reshape x1, local copies, waits for them, and re-layouts, shards(): coarse.reshape(1, n_box * nb, layers * rows_y * rows_x // 8)  0.96 us

profile of v4, /device:TPU:0, one launch (start us, length us, event | category | flops | bytes accessed | tf_op | source)
XLA Modules:
  0.0 30.2 jit_solution(15431912560030520689)
XLA Ops:
  0.6 26.0 %poisson.1 = (bf16[3,4,256,128]{3,2,1,0:T(8,128)(2,1)}, f32[1280,128]{1,0:T(8,128)}) custom-call(s32[5]{0:T(128)} %bitcast.15, bf16[1024,160]{1,0:T(8,128)(2,1)} %bitcast.13, bf16[1024,160]{1,0:T(8,128)(2,1)} %bitcast.14), custom_call_target="tpu_custom_call" | custom-call | tf_op jit(solution)/shard_map/poisson/pallas_call | solution.py:549
  26.6 0.0 copy-start
  26.6 2.6 %reshape.22 = bf16[3,4,32768]{2,1,0:T(4,128)(2,1)} reshape(bf16[3,4,256,128]{3,2,1,0:T(8,128)(2,1)} %get-tuple-element.4) | data formatting | bytes 1572864 | tf_op jit(solution)/shard_map/reshape | solution.py:604
  29.3 0.0 copy-done
  29.3 1.0 %reshape.23 = f32[1,40,4096]{2,1,0:T(8,128)} reshape(f32[1280,128]{1,0:T(8,128)S(1)} %copy-done) | data formatting | bytes 1310720 | tf_op jit(solution)/shard_map/reshape | solution.py:605
Async XLA Ops:
  26.6 2.6 %copy-start = (f32[1280,128]{1,0:T(8,128)S(1)}, f32[1280,128]{1,0:T(8,128)}, u32[]{:S(2)}) copy-start(f32[1280,128]{1,0:T(8,128)} %get-tuple-element.5) | copy-start | bytes 1966084
